TPU v7x, 32 devices: a whole 2x2x4 slice. The times are simulated.
32 devices in a mesh: dp: 8 (over z, x), tensor: 4 (over y, core).
Axes of the slice: x: 2, y: 2, z: 4, core: 2. Of those that a mesh axis runs over, the one named last changes fastest.
Arguments:
- tokens: bfloat16 [4096, 1024], P(('dp', 'tensor')), may hold values from -6 to 6
- seq_lengths: int32 [4], replicated, may hold values from 1 to 2048, 4096 in all
- norm_gain: float32 [1024], replicated, may hold values from 0.5 to 1.5
- mamba_in: bfloat16 [2, 1024, 1536], P(None, 'dp', 'tensor'), may hold values from -0.1875 to 0.1875
- dt_proj: bfloat16 [1024, 24], P('dp', 'tensor'), may hold values from -0.1875 to 0.1875
- bc_proj: bfloat16 [1024, 256], P('dp'), may hold values from -0.1875 to 0.1875
- conv_main: float32 [4, 1536], P(None, 'tensor'), may hold values from -3 to 3
- conv_shared: float32 [4, 256], replicated, may hold values from -3 to 3
- decay_log: float32 [24], P('tensor'), may hold values from -4 to 1.5
- dt_bias: float32 [24], P('tensor'), may hold values from -6 to -2
- skip_gain: float32 [24], P('tensor'), may hold values from 0.5 to 1.5
- gated_gain: float32 [1536], P('tensor'), may hold values from 0.5 to 1.5
- mamba_out: bfloat16 [1536, 1024], P('tensor', 'dp'), may hold values from -0.15625 to 0.15625
- query_proj: bfloat16 [1024, 512], P('dp', 'tensor'), may hold values from -0.1875 to 0.1875
- key_value_projection: bfloat16 [1024, 256], P('dp'), may hold values from -0.1875 to 0.1875
- attn_out: bfloat16 [512, 1024], P('tensor', 'dp'), may hold values from -4 to 4
- ffn_gain: float32 [1024], replicated, may hold values from 0.5 to 1.5
- ffn_in: bfloat16 [2, 1024, 2048], P(None, 'dp', 'tensor'), may hold values from -0.1875 to 0.1875
- ffn_down: bfloat16 [2048, 1024], P('tensor', 'dp'), may hold values from -0.125 to 0.125
- out_grad: bfloat16 [4096, 1024], P(('dp', 'tensor')), may hold values from -6 to 6
Outputs:
- layer_out: bfloat16 [4096, 1024], P(('dp', 'tensor'))
- grad_tokens: float32 [4096, 1024], P(('dp', 'tensor'))
- grad_norm_gain: float32 [1024], replicated
- grad_mamba_in: float32 [2, 1024, 1536], P(None, 'dp', 'tensor')
- grad_dt_proj: float32 [1024, 24], P('dp', 'tensor')
- grad_bc_proj: float32 [1024, 256], P('dp', 'tensor')
- grad_conv_main: float32 [4, 1536], P(None, 'tensor')
- grad_conv_shared: float32 [4, 256], replicated
- grad_decay_log: float32 [24], P('tensor')
- grad_dt_bias: float32 [24], P('tensor')
- grad_skip_gain: float32 [24], P('tensor')
- grad_gated_gain: float32 [1536], P('tensor')
- grad_mamba_out: float32 [1536, 1024], P('tensor', 'dp')
- grad_query_proj: float32 [1024, 512], P('dp', 'tensor')
- grad_kv_proj: float32 [1024, 256], P('dp', 'tensor')
- grad_attn_out: float32 [512, 1024], P('tensor', 'dp')
- grad_ffn_gain: float32 [1024], replicated
- grad_ffn_in: float32 [2, 1024, 2048], P(None, 'dp', 'tensor')
- grad_ffn_down: float32 [2048, 1024], P('tensor', 'dp')
Inputs may be any that keep to these rules, and one draw needn't show every extreme that they name: `seq_lengths`: lengths of the 4 sequences packed in order; they sum to 4096 and the longest is 2048.
All inputs are finite; a program needn't handle non-finite values.
Results may differ from a plain program's by a relative error of at most 0.012.
The roundings to bfloat16 on the way count: a program that leaves them out, or rounds other values in their place, can miss the bound.
Values may be sent and summed in bfloat16 or wider, within the bound.
A program may use at most 192 MiB of HBM per device.

v0:
```python
from functools import partial

import jax
import jax.numpy as jnp
from jax import lax
from jax.sharding import PartitionSpec as P

QUERY_HEADS = 8
KEY_VALUE_HEADS = 2
HEAD_DIMENSION = 64
MAXLEN = 2048
DS = 1536


HIGHEST = lax.Precision.HIGHEST
EPSILON = 1e-05
ROTARY_BASE = 100000000000.0
MASKED = -1e30


def prefix(part, axis, combine, identity, reverse):
    count = lax.axis_size(axis)
    place = lax.axis_index(axis)
    ahead = count - 1 - place if reverse else place
    gathered = jax.tree.map(lambda a: lax.all_gather(a, axis), part)
    state = jax.tree.map(lambda a, e: jnp.zeros_like(a) + jnp.asarray(e, a.dtype), part, identity)

    def one(step, state):
        source = count - 1 - step if reverse else step
        return combine(
            state, jax.tree.map(lambda a: lax.dynamic_index_in_dim(a, source, 0, False), gathered)
        )

    return lax.fori_loop(0, ahead, one, state)


def passed_along(value, axis, steps):
    count = lax.axis_size(axis)
    leading, last = (max(0, -steps), min(count, count - steps))
    return lax.ppermute(value, axis, [(source, source + steps) for source in range(leading, last)])


def layout(lengths, first, length):
    starts = jnp.cumsum(lengths) - lengths
    token_ids = first + jnp.arange(length, dtype=jnp.int32)
    segment = jnp.sum((starts[None, :] <= token_ids[:, None]).astype(jnp.int32), axis=1) - 1
    owner = jnp.arange(starts.shape[0], dtype=jnp.int32)[None, :] == segment[:, None]
    position = token_ids - jnp.sum(jnp.where(owner, starts[None, :], 0), axis=1)
    return (segment, position)


def rms_rows(value_rows, scale):
    return (
        value_rows
        * lax.rsqrt(jnp.mean(value_rows * value_rows, axis=-1, keepdims=True) + EPSILON)
        * scale
    )


def softplus(value_rows):
    return jnp.maximum(value_rows, 0.0) + jnp.log1p(jnp.exp(-jnp.abs(value_rows)))


def silu(value_rows):
    return value_rows * lax.logistic(value_rows)


def rotary(value_rows, position, sign):
    half = value_rows.shape[-1] // 2
    freqs = ROTARY_BASE ** (-2.0 * jnp.arange(half, dtype=jnp.float32) / value_rows.shape[-1])
    angle = position.astype(jnp.float32)[:, None] * freqs[None, :]
    cosine = jnp.cos(angle)[:, None, :]
    sine = sign * jnp.sin(angle)[:, None, :]
    first_half = value_rows[..., :half]
    second_half = value_rows[..., half:]
    return jnp.concatenate(
        [first_half * cosine - second_half * sine, second_half * cosine + first_half * sine],
        axis=-1,
    )


def causal_conv(extended, weight, seg_ext, length):
    lead = weight.shape[0] - 1
    result = weight[0] * extended[lead:]
    for offset in range(1, weight.shape[0]):
        moved = extended[lead - offset : lead - offset + length]
        same = seg_ext[lead - offset : lead - offset + length] == seg_ext[lead:]
        result = result + weight[offset] * jnp.where(same[:, None], moved, 0.0)
    return result


def ssd_block(carry_state, inputs):
    inner, shared_b, shared_c, step_sizes, log_rates, segment, before = inputs
    running = jnp.cumsum(log_rates, axis=0)
    length = step_sizes.shape[0]
    row_ids = jnp.arange(length, dtype=jnp.int32)
    allowed = (segment[:, None] == segment[None, :]) & (row_ids[:, None] >= row_ids[None, :])
    log_gaps = running[:, None, :] - running[None, :, :]
    decays = jnp.exp(jnp.where(allowed[:, :, None], log_gaps, MASKED))
    intersection = jnp.dot(shared_c, shared_b.T, precision=HIGHEST)
    weights = decays * intersection[:, :, None] * step_sizes[None, :, :]
    output = jnp.einsum("ijh,jhp->ihp", weights, inner, precision=HIGHEST)
    carried = jnp.exp(running) * (segment == before)[:, None]
    output = output + carried[:, :, None] * jnp.einsum(
        "hpn,in->ihp", carry_state, shared_c, precision=HIGHEST
    )
    tail_weight = (
        jnp.exp(running[-1][None, :] - running) * (segment == segment[-1])[:, None] * step_sizes
    )
    keep_rate = jnp.exp(running[-1]) * (segment[-1] == before)
    carry_state = keep_rate[:, None, None] * carry_state + jnp.einsum(
        "jh,jhp,jn->hpn", tail_weight, inner, shared_b, precision=HIGHEST
    )
    return (carry_state, output)


def mamba_inputs(
    mixer_ext, shared_ext, step_raw, conv_main, conv_shared, decay_log, dt_bias, seg_ext, heads
):
    length = step_raw.shape[0]
    conv_x = silu(causal_conv(mixer_ext, conv_main, seg_ext, length))
    conv_bc = silu(causal_conv(shared_ext, conv_shared, seg_ext, length))
    states = conv_bc.shape[1] // 2
    step_sizes = softplus(step_raw + dt_bias)
    log_rates = -jnp.exp(decay_log) * step_sizes
    return (
        conv_x.reshape(length, heads, -1),
        conv_bc[:, :states],
        conv_bc[:, states:],
        step_sizes,
        log_rates,
    )


def local_scan(inner, shared_b, shared_c, step_sizes, log_rates, segment, before, block):
    length = step_sizes.shape[0]
    blocks = length // block
    block_before = jnp.concatenate([before[None], segment[:-1]])
    pieces = (
        inner.reshape(blocks, block, inner.shape[1], inner.shape[2]),
        shared_b.reshape(blocks, block, -1),
        shared_c.reshape(blocks, block, -1),
        step_sizes.reshape(blocks, block, -1),
        log_rates.reshape(blocks, block, -1),
        segment.reshape(blocks, block),
        block_before.reshape(blocks, block)[:, 0],
    )
    start_state = jnp.zeros((inner.shape[1], inner.shape[2], shared_b.shape[1]), jnp.float32)
    final_state, output = lax.scan(jax.checkpoint(ssd_block), start_state, pieces)
    carry_rate = jnp.exp(jnp.sum(log_rates, axis=0)) * (segment[-1] == before)
    return (output.reshape(inner.shape), carry_rate, final_state)


def mamba_output(
    local_out, state_in, inner, shared_c, log_rates, skip_gain, gate_z, segment, before
):
    running = jnp.cumsum(log_rates, axis=0)
    carried = jnp.exp(running) * (segment == before)[:, None]
    result = local_out + carried[:, :, None] * jnp.einsum(
        "hpn,in->ihp", state_in, shared_c, precision=HIGHEST
    )
    result = result + skip_gain[None, :, None] * inner
    gated = result.reshape(gate_z.shape) * silu(gate_z)
    return (gated, jnp.sum(gated * gated, axis=1))


def gated_norm(gated, squares, gated_gain):
    return gated * lax.rsqrt(squares[:, None] / DS + EPSILON) * gated_gain


def attend_block(query_blk, key_rows, value_rows, allowed, scale):
    scores = (
        jnp.einsum("qgd,kd->gqk", query_blk, key_rows, preferred_element_type=jnp.float32) * scale
    )
    scores = jnp.where(allowed[None], scores, MASKED)
    row_max = jnp.max(scores, axis=-1, keepdims=True)
    shifted = jnp.exp(scores - row_max)
    row_total = jnp.sum(shifted, axis=-1, keepdims=True)
    probs = (shifted / row_total).astype(jnp.bfloat16)
    output = jnp.einsum("gqk,kd->qgd", probs, value_rows, preferred_element_type=jnp.float32)
    return (output, (row_max + jnp.log(row_total))[..., 0])


def attend_back(query_blk, key_rows, value_rows, allowed, scale, row_lse, grad_out):
    scores = (
        jnp.einsum("qgd,kd->gqk", query_blk, key_rows, preferred_element_type=jnp.float32) * scale
    )
    scores = jnp.where(allowed[None], scores, MASKED)
    probs = jnp.exp(scores - row_lse[..., None])
    grad_values = jnp.einsum(
        "gqk,qgd->kd", probs.astype(jnp.bfloat16), grad_out, preferred_element_type=jnp.float32
    )
    grad_probs = jnp.einsum("qgd,kd->gqk", grad_out, value_rows, preferred_element_type=jnp.float32)
    inner_sum = jnp.sum(grad_probs * probs, axis=-1, keepdims=True)
    grad_scores = (probs * (grad_probs - inner_sum)).astype(jnp.bfloat16) * scale
    grad_query = jnp.einsum(
        "gqk,kd->qgd", grad_scores, key_rows, preferred_element_type=jnp.float32
    )
    grad_keys = jnp.einsum(
        "gqk,qgd->kd", grad_scores, query_blk, preferred_element_type=jnp.float32
    )
    return (grad_query, grad_keys, grad_values)


def per_device(
    tokens,
    seq_lengths,
    norm_gain,
    mamba_in,
    dt_proj,
    bc_proj,
    conv_main,
    conv_shared,
    decay_log,
    dt_bias,
    skip_gain,
    gated_gain,
    mamba_out,
    query_proj,
    key_value_projection,
    attn_out,
    ffn_gain,
    ffn_in,
    ffn_down,
    out_grad,
):
    tensor_size = lax.axis_size("tensor")
    tensor_position = lax.axis_index("tensor")
    group_at = lax.axis_index("dp")
    own_rows = tokens.shape[0]
    group_rows = own_rows * tensor_size
    first_row = group_at * group_rows
    lead = conv_main.shape[0] - 1
    hops = (MAXLEN + group_rows - 2) // group_rows
    scan_block = min(128, group_rows)
    local_heads = decay_log.shape[0]
    query_head_rows = query_proj.shape[1] // HEAD_DIMENSION
    key_value_head = tensor_position * query_head_rows // (QUERY_HEADS // KEY_VALUE_HEADS)
    scale = HEAD_DIMENSION ** (-0.5)
    segment, position = layout(seq_lengths, first_row, group_rows)
    before = layout(seq_lengths, first_row - 1, 1)[0][0]
    seg_ext = layout(seq_lengths, first_row - lead, group_rows + lead)[0]
    key_first = first_row - hops * group_rows
    key_seg = layout(seq_lengths, key_first, (hops + 1) * group_rows)[0]
    key_index = key_first + jnp.arange((hops + 1) * group_rows, dtype=jnp.int32)
    query_index = first_row + jnp.arange(group_rows, dtype=jnp.int32)

    def spread(own_part):
        return lax.all_gather(own_part, "tensor", axis=0, tiled=True)

    def summed_rows(group_part):
        return lax.psum_scatter(group_part, "tensor", scatter_dimension=0, tiled=True)

    def tensor_total(row_values):
        return lax.psum(row_values, "tensor")

    def pass_states(rates, states, step):

        def link_pair(earlier, later):
            return (earlier[0] * later[0], later[0][:, None, None] * earlier[1] + later[1])

        return prefix(
            (rates, states),
            "dp",
            link_pair,
            (jnp.ones_like(rates), jnp.zeros_like(states)),
            step < 0,
        )[1]

    def block_mask():
        return (key_seg[None, :] == segment[:, None]) & (key_index[None, :] <= query_index[:, None])

    gathered = (
        lax.all_gather(mamba_in, "dp", axis=1, tiled=True),
        lax.all_gather(dt_proj, "dp", axis=0, tiled=True),
        lax.all_gather(bc_proj, "dp", axis=0, tiled=True),
        lax.all_gather(query_proj, "dp", axis=0, tiled=True),
        lax.all_gather(key_value_projection, "dp", axis=0, tiled=True),
        lax.all_gather(mamba_out, "dp", axis=1, tiled=True),
        lax.all_gather(attn_out, "dp", axis=1, tiled=True),
        lax.all_gather(ffn_in, "dp", axis=1, tiled=True),
        lax.all_gather(ffn_down, "dp", axis=1, tiled=True),
    )
    (
        full_mamba_in,
        full_dt,
        full_bc,
        full_query,
        gathered_key_value,
        full_mamba_out,
        full_attn_out,
        full_ffn_in,
        full_ffn_down,
    ) = gathered
    normed_own, pull_norm_one = jax.vjp(rms_rows, tokens.astype(jnp.float32), norm_gain)
    normed = spread(normed_own.astype(jnp.bfloat16))
    projected = jnp.einsum(
        "td,sdc->stc", normed, full_mamba_in, preferred_element_type=jnp.float32
    ).astype(jnp.bfloat16)
    gate_z = projected[0]
    mixer_x = projected[1]
    shared_bc = jnp.dot(normed, full_bc, preferred_element_type=jnp.float32).astype(jnp.bfloat16)
    step_raw = jnp.dot(normed, full_dt, preferred_element_type=jnp.float32)
    query_raw = jnp.dot(normed, full_query, preferred_element_type=jnp.float32)
    kv_cols = jnp.concatenate(
        [
            lax.dynamic_slice_in_dim(
                gathered_key_value, key_value_head * HEAD_DIMENSION, HEAD_DIMENSION, 1
            ),
            lax.dynamic_slice_in_dim(
                gathered_key_value,
                (KEY_VALUE_HEADS + key_value_head) * HEAD_DIMENSION,
                HEAD_DIMENSION,
                1,
            ),
        ],
        axis=1,
    )
    key_value_unnormed = jnp.dot(normed, kv_cols, preferred_element_type=jnp.float32)
    queries = rotary(
        query_raw.reshape(group_rows, query_head_rows, HEAD_DIMENSION), position, 1.0
    ).astype(jnp.bfloat16)
    key_rows = rotary(key_value_unnormed[:, None, :HEAD_DIMENSION], position, 1.0)[:, 0].astype(
        jnp.bfloat16
    )
    value_rows = key_value_unnormed[:, HEAD_DIMENSION:].astype(jnp.bfloat16)
    tails = passed_along((mixer_x[-lead:], shared_bc[-lead:]), "dp", 1)
    mixer_ext = jnp.concatenate([tails[0], mixer_x]).astype(jnp.float32)
    shared_ext = jnp.concatenate([tails[1], shared_bc]).astype(jnp.float32)
    prepared, pull_inputs = jax.vjp(
        partial(mamba_inputs, seg_ext=seg_ext, heads=local_heads),
        mixer_ext,
        shared_ext,
        step_raw,
        conv_main,
        conv_shared,
        decay_log,
        dt_bias,
    )
    inner, shared_b, shared_c, step_sizes, log_rates = prepared
    scanned, pull_scan = jax.vjp(
        partial(local_scan, segment=segment, before=before, block=scan_block),
        inner,
        shared_b,
        shared_c,
        step_sizes,
        log_rates,
    )
    local_out, carry_rate, final_state = scanned
    state_in = pass_states(carry_rate, final_state, 1)
    after, pull_after = jax.vjp(
        partial(mamba_output, segment=segment, before=before),
        local_out,
        state_in,
        inner,
        shared_c,
        log_rates,
        skip_gain,
        gate_z.astype(jnp.float32),
    )
    gated, own_squares = after
    squares = tensor_total(own_squares)
    mamba_norm, pull_gated = jax.vjp(gated_norm, gated, squares, gated_gain)
    mamba_low = mamba_norm.astype(jnp.bfloat16)
    arrived = []
    for distance in range(hops, 0, -1):
        arrived.append(passed_along((key_rows, value_rows), "dp", distance))
    all_keys = jnp.concatenate([piece[0] for piece in arrived] + [key_rows])
    all_values = jnp.concatenate([piece[1] for piece in arrived] + [value_rows])
    output, row_lse = attend_block(queries, all_keys, all_values, block_mask(), scale)
    heads_out = output.reshape(group_rows, query_head_rows * HEAD_DIMENSION).astype(jnp.bfloat16)
    mixed_part = jnp.dot(mamba_low, full_mamba_out, preferred_element_type=jnp.float32)
    mixed_part = mixed_part + jnp.dot(heads_out, full_attn_out, preferred_element_type=jnp.float32)
    middle = tokens.astype(jnp.float32) + summed_rows(mixed_part)
    normed_two_own, pull_norm_two = jax.vjp(rms_rows, middle, ffn_gain)
    normed_two = spread(normed_two_own.astype(jnp.bfloat16))
    gate_up = jnp.einsum(
        "td,sdf->stf", normed_two, full_ffn_in, preferred_element_type=jnp.float32
    ).astype(jnp.bfloat16)
    gate_val = gate_up[0].astype(jnp.float32)
    up_val = gate_up[1].astype(jnp.float32)
    hidden = (silu(gate_val) * up_val).astype(jnp.bfloat16)
    layer_out = (
        middle + summed_rows(jnp.dot(hidden, full_ffn_down, preferred_element_type=jnp.float32))
    ).astype(jnp.bfloat16)
    grad_full = spread(out_grad)
    grad_ffn_down = jnp.einsum("tf,td->fd", hidden, grad_full, preferred_element_type=jnp.float32)
    grad_hidden = jnp.einsum(
        "td,fd->tf", grad_full, full_ffn_down, preferred_element_type=jnp.float32
    )
    sigma = lax.logistic(gate_val)
    grad_gate_up = jnp.stack(
        [
            grad_hidden * up_val * sigma * (1.0 + gate_val * (1.0 - sigma)),
            grad_hidden * gate_val * sigma,
        ]
    ).astype(jnp.bfloat16)
    grad_ffn_in = jnp.einsum(
        "td,stf->sdf", normed_two, grad_gate_up, preferred_element_type=jnp.float32
    )
    grad_normed_two = summed_rows(
        jnp.einsum("stf,sdf->td", grad_gate_up, full_ffn_in, preferred_element_type=jnp.float32)
    )
    grad_middle_norm, grad_ffn_gain = pull_norm_two(grad_normed_two)
    grad_middle = out_grad.astype(jnp.float32) + grad_middle_norm
    grad_mixed = spread(grad_middle.astype(jnp.bfloat16))
    grad_mamba_out = jnp.einsum(
        "tc,td->cd", mamba_low, grad_mixed, preferred_element_type=jnp.float32
    )
    grad_attn_out = jnp.einsum(
        "tc,td->cd", heads_out, grad_mixed, preferred_element_type=jnp.float32
    )
    grad_mamba_norm = jnp.einsum(
        "td,cd->tc", grad_mixed, full_mamba_out, preferred_element_type=jnp.float32
    )
    grad_heads = jnp.einsum(
        "td,cd->tc", grad_mixed, full_attn_out, preferred_element_type=jnp.float32
    )
    grad_heads = grad_heads.astype(jnp.bfloat16).reshape(
        group_rows, query_head_rows, HEAD_DIMENSION
    )
    grad_gated, grad_squares, grad_gated_gain = pull_gated(grad_mamba_norm)
    grad_own_squares = tensor_total(grad_squares)
    after_grads = pull_after((grad_gated, grad_own_squares))
    (
        grad_local_out,
        grad_state_in,
        grad_inner_out,
        grad_shared_c_out,
        grad_log_out,
        grad_skip_gain,
        grad_gate_z,
    ) = after_grads
    grad_final = pass_states(carry_rate, grad_state_in, -1)
    grad_carry = jnp.sum(grad_final * state_in, axis=(1, 2))
    scan_grads = pull_scan((grad_local_out, grad_carry, grad_final))
    grad_prepared = (
        scan_grads[0] + grad_inner_out,
        scan_grads[1],
        scan_grads[2] + grad_shared_c_out,
        scan_grads[3],
        scan_grads[4] + grad_log_out,
    )
    input_grads = pull_inputs(grad_prepared)
    (
        grad_mixer_ext,
        grad_shared_ext,
        grad_step_raw,
        grad_conv_main,
        grad_conv_shared,
        grad_decay_log,
        grad_dt_bias,
    ) = input_grads
    returned = passed_along((grad_mixer_ext[:lead], grad_shared_ext[:lead]), "dp", -1)
    grad_mixer_x = jnp.concatenate(
        [grad_mixer_ext[lead:-lead], grad_mixer_ext[-lead:] + returned[0]]
    )
    grad_shared_part = jnp.concatenate(
        [grad_shared_ext[lead:-lead], grad_shared_ext[-lead:] + returned[1]]
    )
    grad_query, grad_keys, grad_values = attend_back(
        queries, all_keys, all_values, block_mask(), scale, row_lse, grad_heads
    )
    grad_keys_own = grad_keys[hops * group_rows :]
    local_value_gradient = grad_values[hops * group_rows :]
    for distance in range(hops, 0, -1):
        slot = hops - distance
        sent_back = passed_along(
            (
                grad_keys[slot * group_rows : (slot + 1) * group_rows],
                grad_values[slot * group_rows : (slot + 1) * group_rows],
            ),
            "dp",
            -distance,
        )
        grad_keys_own = grad_keys_own + sent_back[0]
        local_value_gradient = local_value_gradient + sent_back[1]
    grad_query_raw = rotary(grad_query, position, -1.0).reshape(group_rows, -1).astype(jnp.bfloat16)
    grad_key_raw = rotary(grad_keys_own[:, None, :], position, -1.0)[:, 0]
    key_value_gradient_full = jnp.zeros((group_rows, gathered_key_value.shape[1]), jnp.float32)
    key_value_gradient_full = lax.dynamic_update_slice_in_dim(
        key_value_gradient_full, grad_key_raw, key_value_head * HEAD_DIMENSION, 1
    )
    key_value_gradient_full = lax.dynamic_update_slice_in_dim(
        key_value_gradient_full,
        local_value_gradient,
        (KEY_VALUE_HEADS + key_value_head) * HEAD_DIMENSION,
        1,
    )
    shared = lax.psum((grad_shared_part, key_value_gradient_full), "tensor")
    bc_width = full_bc.shape[1] // tensor_size
    kv_width = gathered_key_value.shape[1] // tensor_size
    grad_bc_block = lax.dynamic_slice_in_dim(
        shared[0].astype(jnp.bfloat16), tensor_position * bc_width, bc_width, 1
    )
    grad_kv_block = lax.dynamic_slice_in_dim(
        shared[1].astype(jnp.bfloat16), tensor_position * kv_width, kv_width, 1
    )
    bc_block = lax.dynamic_slice_in_dim(full_bc, tensor_position * bc_width, bc_width, 1)
    kv_block = lax.dynamic_slice_in_dim(gathered_key_value, tensor_position * kv_width, kv_width, 1)
    grad_proj = jnp.stack([grad_gate_z, grad_mixer_x]).astype(jnp.bfloat16)
    grad_step_low = grad_step_raw.astype(jnp.bfloat16)
    grad_mamba_in = jnp.einsum("td,stc->sdc", normed, grad_proj, preferred_element_type=jnp.float32)
    grad_dt_proj = jnp.einsum(
        "td,th->dh", normed, grad_step_low, preferred_element_type=jnp.float32
    )
    grad_query_proj = jnp.einsum(
        "td,tc->dc", normed, grad_query_raw, preferred_element_type=jnp.float32
    )
    grad_bc_proj = jnp.einsum(
        "td,tc->dc", normed, grad_bc_block, preferred_element_type=jnp.float32
    )
    grad_kv_proj = jnp.einsum(
        "td,tc->dc", normed, grad_kv_block, preferred_element_type=jnp.float32
    )
    grad_normed = jnp.einsum(
        "stc,sdc->td", grad_proj, full_mamba_in, preferred_element_type=jnp.float32
    )
    grad_normed = grad_normed + jnp.einsum(
        "th,dh->td", grad_step_low, full_dt, preferred_element_type=jnp.float32
    )
    grad_normed = grad_normed + jnp.einsum(
        "tc,dc->td", grad_query_raw, full_query, preferred_element_type=jnp.float32
    )
    grad_normed = grad_normed + jnp.einsum(
        "tc,dc->td", grad_bc_block, bc_block, preferred_element_type=jnp.float32
    )
    grad_normed = grad_normed + jnp.einsum(
        "tc,dc->td", grad_kv_block, kv_block, preferred_element_type=jnp.float32
    )
    grad_normed_own = summed_rows(grad_normed)
    grad_tokens_norm, grad_norm_gain = pull_norm_one(grad_normed_own)
    grad_tokens = grad_middle + grad_tokens_norm
    scattered = (
        lax.psum_scatter(grad_mamba_in, "dp", scatter_dimension=1, tiled=True),
        lax.psum_scatter(grad_dt_proj, "dp", scatter_dimension=0, tiled=True),
        lax.psum_scatter(grad_bc_proj, "dp", scatter_dimension=0, tiled=True),
        lax.psum_scatter(grad_query_proj, "dp", scatter_dimension=0, tiled=True),
        lax.psum_scatter(grad_kv_proj, "dp", scatter_dimension=0, tiled=True),
        lax.psum_scatter(grad_mamba_out, "dp", scatter_dimension=1, tiled=True),
        lax.psum_scatter(grad_attn_out, "dp", scatter_dimension=1, tiled=True),
        lax.psum_scatter(grad_ffn_in, "dp", scatter_dimension=1, tiled=True),
        lax.psum_scatter(grad_ffn_down, "dp", scatter_dimension=1, tiled=True),
    )

    def widen(piece, axis_at):
        new_shape = list(piece.shape)
        new_shape[axis_at] = new_shape[axis_at] * tensor_size
        return lax.dynamic_update_slice_in_dim(
            jnp.zeros(new_shape, jnp.float32),
            piece,
            tensor_position * piece.shape[axis_at],
            axis_at,
        )

    def narrow(whole, axis_at, width):
        return lax.dynamic_slice_in_dim(whole, tensor_position * width, width, axis_at)

    small = lax.psum(
        (
            grad_norm_gain,
            grad_ffn_gain,
            grad_conv_shared,
            widen(grad_conv_main, 1),
            widen(grad_decay_log, 0),
            widen(grad_dt_bias, 0),
            widen(grad_skip_gain, 0),
            widen(grad_gated_gain, 0),
        ),
        ("dp", "tensor"),
    )
    return (
        layer_out,
        grad_tokens,
        small[0],
        scattered[0],
        scattered[1],
        scattered[2],
        narrow(small[3], 1, conv_main.shape[1]),
        small[2],
        narrow(small[4], 0, local_heads),
        narrow(small[5], 0, local_heads),
        narrow(small[6], 0, local_heads),
        narrow(small[7], 0, gated_gain.shape[0]),
        scattered[5],
        scattered[3],
        scattered[4],
        scattered[6],
        small[1],
        scattered[7],
        scattered[8],
    )


def solution(mesh):
    return jax.shard_map(
        per_device,
        mesh=mesh,
        in_specs=(
            P(("dp", "tensor"), None),
            P(),
            P(),
            P(None, "dp", "tensor"),
            P("dp", "tensor"),
            P("dp", None),
            P(None, "tensor"),
            P(),
            P("tensor"),
            P("tensor"),
            P("tensor"),
            P("tensor"),
            P("tensor", "dp"),
            P("dp", "tensor"),
            P("dp", None),
            P("tensor", "dp"),
            P(),
            P(None, "dp", "tensor"),
            P("tensor", "dp"),
            P(("dp", "tensor"), None),
        ),
        out_specs=(
            P(("dp", "tensor"), None),
            P(("dp", "tensor"), None),
            P(),
            P(None, "dp", "tensor"),
            P("dp", "tensor"),
            P("dp", "tensor"),
            P(None, "tensor"),
            P(),
            P("tensor"),
            P("tensor"),
            P("tensor"),
            P("tensor"),
            P("tensor", "dp"),
            P("dp", "tensor"),
            P("dp", "tensor"),
            P("tensor", "dp"),
            P(),
            P(None, "dp", "tensor"),
            P("tensor", "dp"),
        ),
        check_vma=False,
    )
```

profile of v0, /device:TPU:0, one launch (start us, length us, event | category | flops | bytes accessed | tf_op | source)
XLA Modules:
  0.0 1672.0 jit_solution(13644495777177104574)
XLA Ops:
  15.6 33.9 %all_gather.60 = bf16[1024,256]{1,0:T(8,128)(2,1)S(1)} all-gather(bf16[128,256]{1,0:T(8,128)(2,1)} %param.33), channel_id=1, replica_groups=mesh['dp'=8,'tensor'=4] {'dp'}, dimensions={0}, use_global_device_ids=true | all-gather | bytes 589824 | tf_op jit(solution)/shard_map/all_gather | solution.py:276
  51.8 26.3 %all_gather.58 = bf16[1024,6]{0,1:T(8,128)(2,1)S(1)} all-gather(bf16[128,6]{0,1:T(8,128)(2,1)} %param.32), channel_id=1, replica_groups=mesh['dp'=8,'tensor'=4] {'dp'}, dimensions={0}, use_global_device_ids=true | all-gather | bytes 13824 | tf_op jit(solution)/shard_map/all_gather | solution.py:275
  79.4 31.4 %all_gather.65 = bf16[1024,256]{1,0:T(8,128)(2,1)S(1)} all-gather(bf16[128,256]{1,0:T(8,128)(2,1)} %param.42), channel_id=1, replica_groups=mesh['dp'=8,'tensor'=4] {'dp'}, dimensions={0}, use_global_device_ids=true | all-gather | bytes 589824 | tf_op jit(solution)/shard_map/all_gather | solution.py:278
  110.9 31.0 %all_gather.66 = bf16[1024,128]{1,0:T(8,128)(2,1)S(1)} all-gather(bf16[128,128]{1,0:T(8,128)(2,1)} %param.41), channel_id=1, replica_groups=mesh['dp'=8,'tensor'=4] {'dp'}, dimensions={0}, use_global_device_ids=true | all-gather | bytes 294912 | tf_op jit(solution)/shard_map/all_gather | solution.py:277
  144.9 28.0 %all_gather.67 = bf16[128,1024]{1,0:T(8,128)(2,1)} all-gather(bf16[128,128]{1,0:T(8,128)(2,1)} %param.43), channel_id=1, replica_groups=mesh['dp'=8,'tensor'=4] {'dp'}, dimensions={1}, use_global_device_ids=true | all-gather | bytes 294912 | tf_op jit(solution)/shard_map/all_gather | solution.py:280
  173.0 28.9 %all_gather.64 = bf16[384,1024]{1,0:T(8,128)(2,1)} all-gather(bf16[384,128]{1,0:T(8,128)(2,1)} %param.40), channel_id=1, replica_groups=mesh['dp'=8,'tensor'=4] {'dp'}, dimensions={1}, use_global_device_ids=true | all-gather | bytes 884736 | tf_op jit(solution)/shard_map/all_gather | solution.py:279
  229.7 18.6 %all-reduce.20 = f32[48]{0:T(128)S(1)} all-reduce(f32[48]{0:T(128)S(1)} %multiply_dynamic-update-slice_fusion.1), channel_id=2, replica_groups=mesh['dp'=8,'tensor'=4] {'dp'}, use_global_device_ids=true, to_apply=%add.20 | all-reduce | flops 48 | bytes 384
  286.5 78.8 %while.69 = (s32[]{:T(128)}, f32[6,64,128]{2,1,0:T(8,128)S(1)}, f32[4,128,6,64]{1,0,3,2:T(4,128)}, f32[4,6,64,128]{3,2,1,0:T(8,128)}, f32[4,128,6]{2,1,0:T(8,128...) while((s32[]{:T(128)}, f32[6,64,128]{2,1,0:T(8,128)S(1)}, ...), condition=%wide.region_7.8_spmd.clone, body=%wide.region_5.7_spmd.clone.sunk | while | flops 252594944 | bytes 2863971 | solution.py:149
  382.9 30.6 %all-gather.27.cloned.1.call-done = f32[48,64,128]{2,1,0:T(8,128)} async-done(((f32[6,64,128]{2,1,0:T(8,128)}), f32[48,64,128]{2,1,0:T(8,128)}) %all-gather.27.cloned.1.call-update) | async-done | bytes 1572880 | tf_op jit(solution)/shard_map/all_gather | solution.py:25
  432.4 37.3 %reduce-scatter.14.cloned.1.call-done = f32[128,1024]{1,0:T(8,128)} async-done(((f32[512,1024]{1,0:T(8,128)}), f32[128,1024]{1,0:T(8,128)}) %reduce-scatter.14.cloned.1.call-update) | async-done | bytes 524304 | tf_op jit(solution)/shard_map/reduce_scatter | solution.py:252
  473.3 47.9 %all-gather.19.cloned.1.call-done = bf16[2,1024,512]{2,1,0:T(8,128)(2,1)} async-done(((bf16[2,128,512]{2,1,0:T(8,128)(2,1)}), bf16[2,1024,512]{2,1,0:T(8,128)(2,1)}) %all-gather.19.cloned.1.call-update) | async-done | bytes 2097168 | tf_op jit(solution)/shard_map/all_gather | solution.py:281
  521.2 17.3 %all-gather.17.cloned.1.call-done = bf16[512,1024]{1,0:T(8,128)(2,1)} async-done(((bf16[128,1024]{1,0:T(8,128)(2,1)}), bf16[512,1024]{1,0:T(8,128)(2,1)}) %all-gather.17.cloned.1.call-update) | async-done | bytes 1048592 | tf_op jit(solution)/shard_map/all_gather | solution.py:249
  542.7 14.2 all-gather.23.cloned.1.call-done
  556.9 41.8 %all-gather.21.cloned.1.call-done = bf16[512,1024]{1,0:T(8,128)(2,1)} async-done(((bf16[512,128]{1,0:T(8,128)(2,1)}), bf16[512,1024]{1,0:T(8,128)(2,1)}) %all-gather.21.cloned.1.call-update) | async-done | bytes 1048592 | tf_op jit(solution)/shard_map/all_gather | solution.py:282
  605.5 30.4 %reduce-scatter.18.cloned.1.call-done = f32[128,1024]{1,0:T(8,128)} async-done(((f32[512,1024]{1,0:T(8,128)}), f32[128,1024]{1,0:T(8,128)}) %reduce-scatter.18.cloned.1.call-update) | async-done | bytes 524304 | tf_op jit(solution)/shard_map/reduce_scatter | solution.py:252
  640.0 16.7 all-gather.25.cloned.1.call-done
  698.0 16.2 fusion.92
  714.3 15.6 convolution_bitcast_fusion.5
  750.7 40.7 %collective-permute-done.12 = f32[512,64]{0,1:T(8,128)S(1)} collective-permute-done((f32[512,64]{0,1:T(8,128)S(1)}, f32[512,64]{0,1:T(8,128)S(1)}, u32[]{:S(2)}, u32[]{:S(2)}) %collective-permute-start.12) | collective-permute-done | bytes 131104 | tf_op jit(solution)/shard_map/ppermute | solution.py:40
  816.9 12.2 while.67
  833.0 179.7 %while.68 = (s32[]{:T(128)}, f32[6,64,128]{2,1,0:T(8,128)S(1)}, f32[4,128,6,64]{1,0,3,2:T(4,128)}, f32[4,128,128]{2,1,0:T(8,128)}, f32[4,128,128]{2,1,0:T(8,128)...) while((s32[]{:T(128)}, f32[6,64,128]{2,1,0:T(8,128)S(1)}, ...), condition=%wide.region_38.39_spmd, body=%wide.region_28.38_spmd.sunk | while | flops 606566400 | bytes 7241879 | solution.py:149
  1030.1 26.5 %all-reduce.24 = (bf16[512,256]{1,0:T(8,128)(2,1)}, bf16[512,256]{1,0:T(8,128)(2,1)}) all-reduce(f32[512,256]{1,0:T(8,128)} %copy-done.32, f32[512,256]{1,0:T(8,128)} %pad_maximum_fusion.4), channel_id=1, replica_groups=mesh['dp'=8,'tensor'=4] {'tensor'}, use_global_device_ids=true, to_apply=%region_45.46 | all-reduce | flops 262144 | bytes 1572864 | tf_op jit(solution)/shard_map/psum | solution.py:490
  1087.8 7.9 reduce-scatter.20.cloned.1.call-done
  1096.9 40.6 %all-reduce.21 = (f32[1024]{0:T(1024)}, f32[4,1536]{1,0:T(4,128)S(1)}, f32[4,256]{1,0:T(4,128)}, f32[24]{0:T(128)S(1)}, f32[24]{0:T(128)S(1)}, /*index=5*/f32[24]{0:T(128)S(1)}, f32[1536]{0:T(1024)S(1)}, f32[1024]{0:T(1024)}) all-reduce(f32[1024]{0:T(1024)S(1)} %get-tuple-element.918, ...), channel_id=1, replica_groups=mesh['dp'=8,'tensor'=4] {'dp','tensor'}, use_global_device_ids=true, to_apply=%region_49.50 | all-reduce | flops 10824 | bytes 86592 | tf_op jit(solution)/shard_map/psum | solution.py:559
  1142.9 65.4 %reduce-scatter.22.cloned.1.call-done = f32[2,128,384]{1,2,0:T(8,128)} async-done(((f32[2,1024,384]{1,2,0:T(8,128)}), f32[2,128,384]{1,2,0:T(8,128)}) %reduce-scatter.22.cloned.1.call-update) | async-done | bytes 393232 | tf_op jit(solution)/shard_map/reduce_scatter | solution.py:535
  1210.2 69.6 %reduce-scatter.38.cloned.1.call-done = f32[512,128]{1,0:T(8,128)} async-done(((f32[512,1024]{1,0:T(8,128)}), f32[512,128]{1,0:T(8,128)}) %reduce-scatter.38.cloned.1.call-update) | async-done | bytes 262160 | tf_op jit(solution)/shard_map/reduce_scatter | solution.py:543
  1279.8 65.2 %reduce-scatter.30.cloned.1.call-done = f32[128,128]{1,0:T(8,128)} async-done(((f32[1024,128]{1,0:T(8,128)}), f32[128,128]{1,0:T(8,128)}) %reduce-scatter.30.cloned.1.call-update) | async-done | bytes 65552 | tf_op jit(solution)/shard_map/reduce_scatter | solution.py:538
  1345.0 65.2 %reduce-scatter.34.cloned.1.call-done = f32[128,128]{1,0:T(8,128)} async-done(((f32[128,1024]{1,0:T(8,128)}), f32[128,128]{1,0:T(8,128)}) %reduce-scatter.34.cloned.1.call-update) | async-done | bytes 65552 | tf_op jit(solution)/shard_map/reduce_scatter | solution.py:541
  1410.2 56.6 %reduce-scatter.24.cloned.1.call-done = f32[128,6]{0,1:T(8,128)} async-done(((f32[1024,6]{0,1:T(8,128)}), f32[128,6]{0,1:T(8,128)}) %reduce-scatter.24.cloned.1.call-update) | async-done | bytes 3088 | tf_op jit(solution)/shard_map/reduce_scatter | solution.py:536
  1466.8 68.9 %reduce-scatter.28.cloned.1.call-done = f32[384,128]{1,0:T(8,128)} async-done(((f32[384,1024]{1,0:T(8,128)}), f32[384,128]{1,0:T(8,128)}) %reduce-scatter.28.cloned.1.call-update) | async-done | bytes 196624 | tf_op jit(solution)/shard_map/reduce_scatter | solution.py:540
  1535.8 64.5 %reduce-scatter.26.cloned.1.call-done = f32[128,64]{0,1:T(8,128)} async-done(((f32[1024,64]{0,1:T(8,128)}), f32[128,64]{0,1:T(8,128)}) %reduce-scatter.26.cloned.1.call-update) | async-done | bytes 32784 | tf_op jit(solution)/shard_map/reduce_scatter | solution.py:537
  1600.3 64.6 %reduce-scatter.32.cloned.1.call-done = f32[128,64]{0,1:T(8,128)} async-done(((f32[1024,64]{0,1:T(8,128)}), f32[128,64]{0,1:T(8,128)}) %reduce-scatter.32.cloned.1.call-update) | async-done | bytes 32784 | tf_op jit(solution)/shard_map/reduce_scatter | solution.py:539
  (789 shorter events, 540.0 us)
Async XLA Ops:
  7.2 197.1 %all-gather.13.cloned.1.call-start = ((), (), s32[]{:S(2)}) async-start(), calls=%async_computation.13 | async-start | bytes 1310720 | tf_op jit(solution)/shard_map/all_gather | solution.py:249
  10.2 259.4 %all-gather.15.cloned.1.call-start = ((), (), s32[]{:S(2)}) async-start(), calls=%async_computation.14 | async-start | bytes 1769472 | tf_op jit(solution)/shard_map/all_gather | solution.py:274
  10.9 402.6 %all-gather.27.cloned.1.call-start = ((), (), s32[]{:S(2)}) async-start(), calls=%async_computation.33 | async-start | bytes 1769472 | tf_op jit(solution)/shard_map/all_gather | solution.py:25
  207.9 40.5 %collective-permute-start.1 = (bf16[3,256]{1,0:T(4,128)(2,1)S(1)}, bf16[3,256]{1,0:T(4,128)(2,1)S(1)}, u32[]{:S(2)}, u32[]{:S(2)}) collective-permute-start(bf16[3,256]{1,0:T(4,128)(2,1)S(1)} %slice.302), channel_id=1, source_target_pairs={{0,4},{4,8},{8,12},{12,16},{16,20},{20,24},{24,28},{1,5},{5,9},{9,... | collective-permute-start | bytes 4616 | tf_op jit(solution)/shard_map/ppermute | solution.py:40
  214.2 54.7 %collective-permute-start.2 = (bf16[512,64]{0,1:T(8,128)(2,1)S(1)}, bf16[512,64]{0,1:T(8,128)(2,1)S(1)}, u32[]{:S(2)}, u32[]{:S(2)}) collective-permute-start(bf16[512,64]{0,1:T(8,128)(2,1)S(1)} %slice.473), channel_id=1, source_target_pairs={{0,16},{4,20},{8,24},{12,28},{1,17},{5,21},{9,25},{13,29},{2,18},{... | collective-permute-start | bytes 196616 | tf_op jit(solution)/shard_map/ppermute | solution.py:40
  220.7 48.2 %collective-permute-start.3 = (bf16[512,64]{0,1:T(8,128)(2,1)S(1)}, bf16[512,64]{0,1:T(8,128)(2,1)S(1)}, u32[]{:S(2)}, u32[]{:S(2)}) collective-permute-start(bf16[512,64]{0,1:T(8,128)(2,1)S(1)} %slice.473), channel_id=1, source_target_pairs={{0,12},{4,16},{8,20},{12,24},{16,28},{1,13},{5,17},{9,21},{13,25},... | collective-permute-start | bytes 196616 | tf_op jit(solution)/shard_map/ppermute | solution.py:40
  223.4 45.5 %collective-permute-start.4 = (bf16[512,64]{0,1:T(8,128)(2,1)S(1)}, bf16[512,64]{0,1:T(8,128)(2,1)S(1)}, u32[]{:S(2)}, u32[]{:S(2)}) collective-permute-start(bf16[512,64]{0,1:T(8,128)(2,1)S(1)} %slice.473), channel_id=1, source_target_pairs={{0,8},{4,12},{8,16},{12,20},{16,24},{20,28},{1,9},{5,13},{9,17},{1... | collective-permute-start | bytes 196616 | tf_op jit(solution)/shard_map/ppermute | solution.py:40
  226.9 42.0 %collective-permute-start.5 = (bf16[512,64]{0,1:T(8,128)(2,1)S(1)}, bf16[512,64]{0,1:T(8,128)(2,1)S(1)}, u32[]{:S(2)}, u32[]{:S(2)}) collective-permute-start(bf16[512,64]{0,1:T(8,128)(2,1)S(1)} %slice.473), channel_id=1, source_target_pairs={{0,4},{4,8},{8,12},{12,16},{16,20},{20,24},{24,28},{1,5},{5,9},{9,... | collective-permute-start | bytes 196616 | tf_op jit(solution)/shard_map/ppermute | solution.py:40
  366.0 103.6 %reduce-scatter.14.cloned.1.call-start = ((), (), s32[]{:S(2)}) async-start(), calls=%async_computation.15 | async-start | bytes 2621440 | tf_op jit(solution)/shard_map/reduce_scatter | solution.py:252
  431.7 89.5 %all-gather.19.cloned.1.call-start = ((), (), s32[]{:S(2)}) async-start(), calls=%async_computation.17 | async-start | bytes 2359296 | tf_op jit(solution)/shard_map/all_gather | solution.py:281
  432.3 106.2 %all-gather.17.cloned.1.call-start = ((), (), s32[]{:S(2)}) async-start(), calls=%async_computation.16 | async-start | bytes 1310720 | tf_op jit(solution)/shard_map/all_gather | solution.py:249
  471.7 85.2 %all-gather.23.cloned.1.call-start = ((), (), s32[]{:S(2)}) async-start(), calls=%async_computation.20 | async-start | bytes 1310720 | tf_op jit(solution)/shard_map/all_gather | solution.py:249
  472.5 126.2 %all-gather.21.cloned.1.call-start = ((), (), s32[]{:S(2)}) async-start(), calls=%async_computation.18 | async-start | bytes 1179648 | tf_op jit(solution)/shard_map/all_gather | solution.py:282
  473.2 162.7 %reduce-scatter.18.cloned.1.call-start = ((), (), s32[]{:S(2)}) async-start(), calls=%async_computation.21 | async-start | bytes 2621440 | tf_op jit(solution)/shard_map/reduce_scatter | solution.py:252
  605.4 51.2 %all-gather.25.cloned.1.call-start = ((), (), s32[]{:S(2)}) async-start(), calls=%async_computation.22 | async-start | bytes 1310720 | tf_op jit(solution)/shard_map/all_gather | solution.py:249
  639.7 176.3 %all-gather.29.cloned.1.call-start = ((), (), s32[]{:S(2)}) async-start(), calls=%async_computation.34 | async-start | bytes 1769472 | tf_op jit(solution)/shard_map/all_gather | solution.py:25
  674.4 406.7 %reduce-scatter.36.cloned.1.call-start = ((), (), s32[]{:S(2)}) async-start(), calls=%async_computation.31 | async-start | bytes 4718592 | tf_op jit(solution)/shard_map/reduce_scatter | solution.py:542
  680.1 415.5 %reduce-scatter.20.cloned.1.call-start = ((), (), s32[]{:S(2)}) async-start(), calls=%async_computation.23 | async-start | bytes 2621440 | tf_op jit(solution)/shard_map/reduce_scatter | solution.py:252
  743.5 54.7 %collective-permute-start.16 = (f32[512,64]{1,0:T(8,128)}, f32[512,64]{1,0:T(8,128)}, u32[]{:S(2)}, u32[]{:S(2)}) collective-permute-start(f32[512,64]{1,0:T(8,128)} %get-tuple-element.1045), channel_id=1, source_target_pairs={{16,0},{20,4},{24,8},{28,12},{17,1},{21,5},{25,9},{29,13},{18,2},{... | collective-permute-start | bytes 393224 | tf_op jit(solution)/shard_map/ppermute | solution.py:40
  744.9 46.6 %collective-permute-start.12 = (f32[512,64]{0,1:T(8,128)S(1)}, f32[512,64]{0,1:T(8,128)S(1)}, u32[]{:S(2)}, u32[]{:S(2)}) collective-permute-start(f32[512,64]{0,1:T(8,128)S(1)} %get-tuple-element.1055), channel_id=1, source_target_pairs={{16,0},{20,4},{24,8},{28,12},{17,1},{21,5},{25,9},{29,13},{18,2},{... | collective-permute-start | bytes 393224 | tf_op jit(solution)/shard_map/ppermute | solution.py:40
  746.2 46.6 %collective-permute-start.13 = (f32[512,64]{0,1:T(8,128)S(1)}, f32[512,64]{0,1:T(8,128)S(1)}, u32[]{:S(2)}, u32[]{:S(2)}) collective-permute-start(f32[512,64]{0,1:T(8,128)S(1)} %get-tuple-element.1058), channel_id=1, source_target_pairs={{12,0},{16,4},{20,8},{24,12},{28,16},{13,1},{17,5},{21,9},{25,13},... | collective-permute-start | bytes 393224 | tf_op jit(solution)/shard_map/ppermute | solution.py:40
  747.5 46.6 %collective-permute-start.14 = (f32[512,64]{0,1:T(8,128)S(1)}, f32[512,64]{0,1:T(8,128)S(1)}, u32[]{:S(2)}, u32[]{:S(2)}) collective-permute-start(f32[512,64]{0,1:T(8,128)S(1)} %get-tuple-element.1057), channel_id=1, source_target_pairs={{8,0},{12,4},{16,8},{20,12},{24,16},{28,20},{9,1},{13,5},{17,9},{2... | collective-permute-start | bytes 393224 | tf_op jit(solution)/shard_map/ppermute | solution.py:40
  748.8 47.0 %collective-permute-start.15 = (f32[512,64]{0,1:T(8,128)S(1)}, f32[512,64]{0,1:T(8,128)S(1)}, u32[]{:S(2)}, u32[]{:S(2)}) collective-permute-start(f32[512,64]{0,1:T(8,128)S(1)} %get-tuple-element.1056), channel_id=1, source_target_pairs={{4,0},{8,4},{12,8},{16,12},{20,16},{24,20},{28,24},{5,1},{9,5},{13... | collective-permute-start | bytes 393224 | tf_op jit(solution)/shard_map/ppermute | solution.py:40
  1063.1 77.4 %reduce-scatter.16.cloned.1.call-start = ((), (), s32[]{:S(2)}) async-start(), calls=%async_computation.19 | async-start | bytes 2621440 | tf_op jit(solution)/shard_map/reduce_scatter | solution.py:252
  1066.6 141.7 %reduce-scatter.22.cloned.1.call-start = ((), (), s32[]{:S(2)}) async-start(), calls=%async_computation.24 | async-start | bytes 3538944 | tf_op jit(solution)/shard_map/reduce_scatter | solution.py:535
  1069.4 210.4 %reduce-scatter.38.cloned.1.call-start = ((), (), s32[]{:S(2)}) async-start(), calls=%async_computation.32 | async-start | bytes 2359296 | tf_op jit(solution)/shard_map/reduce_scatter | solution.py:543
  1073.3 271.7 %reduce-scatter.30.cloned.1.call-start = ((), (), s32[]{:S(2)}) async-start(), calls=%async_computation.28 | async-start | bytes 589824 | tf_op jit(solution)/shard_map/reduce_scatter | solution.py:538
  1074.7 335.6 %reduce-scatter.34.cloned.1.call-start = ((), (), s32[]{:S(2)}) async-start(), calls=%async_computation.30 | async-start | bytes 589824 | tf_op jit(solution)/shard_map/reduce_scatter | solution.py:541
  1075.9 391.0 %reduce-scatter.24.cloned.1.call-start = ((), (), s32[]{:S(2)}) async-start(), calls=%async_computation.25 | async-start | bytes 36864 | tf_op jit(solution)/shard_map/reduce_scatter | solution.py:536
  1076.9 458.8 %reduce-scatter.28.cloned.1.call-start = ((), (), s32[]{:S(2)}) async-start(), calls=%async_computation.27 | async-start | bytes 1769472 | tf_op jit(solution)/shard_map/reduce_scatter | solution.py:540
  1080.3 520.0 %reduce-scatter.26.cloned.1.call-start = ((), (), s32[]{:S(2)}) async-start(), calls=%async_computation.26 | async-start | bytes 294912 | tf_op jit(solution)/shard_map/reduce_scatter | solution.py:537
  1085.3 579.6 %reduce-scatter.32.cloned.1.call-start = ((), (), s32[]{:S(2)}) async-start(), calls=%async_computation.29 | async-start | bytes 294912 | tf_op jit(solution)/shard_map/reduce_scatter | solution.py:539
  (129 other events, 6167.6 us)
Sparse Core Ops, SparseCore 0:
  10.3 19.4 all-gather.12
  32.0 45.5 all-gather.14
  366.2 47.2 all-gather.26
  431.8 37.7 reduce-scatter.13
  471.9 49.2 all-gather.18
  523.3 15.2 all-gather.16
  540.1 16.7 all-gather.22
  559.1 39.5 all-gather.20
  605.6 30.3 reduce-scatter.17
  639.8 16.7 all-gather.24
  674.5 45.2 all-gather.28
  723.3 120.7 reduce-scatter.35
  1063.2 32.3 reduce-scatter.19
  1098.0 31.4 reduce-scatter.15
  1133.4 74.8 reduce-scatter.21
  1212.7 67.1 reduce-scatter.37
  1284.0 61.0 reduce-scatter.29
  1348.8 61.3 reduce-scatter.33
  1414.2 52.5 reduce-scatter.23
  1471.1 64.6 reduce-scatter.27
  1539.7 60.5 reduce-scatter.25
  1604.2 60.6 reduce-scatter.31
where the time goes:
time: 1690 us; the launch traced here: 1670 us
  waiting for transfers between devices  829 us (49%)
  blocking collectives  277 us (16%)
  matrix products  189 us (11%)
  local copies, waits for them, and re-layouts  187 us (11%)
  other arithmetic  113 us (7%)
  starting transfers between devices  46.7 us (3%)
  between operations  18.7 us (1%)
    reduce_scatter x4, waiting for transfers between devices, summed_rows(): lax.psum_scatter(group_part, 'tensor', scatter_dimension=0, tiled=True)  75.6 us
    reduce_scatter x1, waiting for transfers between devices, per_device(): lax.psum_scatter(grad_ffn_down, 'dp', scatter_dimension=1, tiled=True)  69.6 us
    reduce_scatter x1, waiting for transfers between devices, per_device(): lax.psum_scatter(grad_mamba_out, 'dp', scatter_dimension=1, tiled=True)  68.9 us
    reduce_scatter x1, waiting for transfers between devices, per_device(): lax.psum_scatter(grad_mamba_in, 'dp', scatter_dimension=1, tiled=True)  65.4 us
    reduce_scatter x1, waiting for transfers between devices, per_device(): lax.psum_scatter(grad_attn_out, 'dp', scatter_dimension=1, tiled=True)  65.2 us
    reduce_scatter x1, waiting for transfers between devices, per_device(): lax.psum_scatter(grad_query_proj, 'dp', scatter_dimension=0, tiled=True)  65.2 us
    reduce_scatter x1, waiting for transfers between devices, per_device(): lax.psum_scatter(grad_kv_proj, 'dp', scatter_dimension=0, tiled=True)  64.6 us
    reduce_scatter x1, waiting for transfers between devices, per_device(): lax.psum_scatter(grad_bc_proj, 'dp', scatter_dimension=0, tiled=True)  64.5 us
  transfers between devices with their start and end apart: 42, of which 25 were waited for; matrix products, arithmetic and copies ran while one was open for 22% of the time, Pallas kernels for 0%

commit v1 on v0

--- a/solution.py
+++ b/solution.py
@@ -270,28 +270,36 @@
     def block_mask():
         return (key_seg[None, :] == segment[:, None]) & (key_index[None, :] <= query_index[:, None])
 
-    gathered = (
-        lax.all_gather(mamba_in, "dp", axis=1, tiled=True),
-        lax.all_gather(dt_proj, "dp", axis=0, tiled=True),
-        lax.all_gather(bc_proj, "dp", axis=0, tiled=True),
-        lax.all_gather(query_proj, "dp", axis=0, tiled=True),
-        lax.all_gather(key_value_projection, "dp", axis=0, tiled=True),
-        lax.all_gather(mamba_out, "dp", axis=1, tiled=True),
-        lax.all_gather(attn_out, "dp", axis=1, tiled=True),
-        lax.all_gather(ffn_in, "dp", axis=1, tiled=True),
-        lax.all_gather(ffn_down, "dp", axis=1, tiled=True),
-    )
-    (
-        full_mamba_in,
-        full_dt,
-        full_bc,
-        full_query,
-        gathered_key_value,
-        full_mamba_out,
-        full_attn_out,
-        full_ffn_in,
-        full_ffn_down,
-    ) = gathered
+    def pack(parts):
+        return jnp.concatenate(parts, axis=1)
+
+    def unpack(packed, widths):
+        pieces, at = [], 0
+        for width in widths:
+            pieces.append(packed[:, at : at + width])
+            at += width
+        return pieces
+
+    first_parts = (
+        mamba_in[0],
+        mamba_in[1],
+        bc_proj,
+        key_value_projection,
+        query_proj,
+        dt_proj,
+    )
+    second_parts = (mamba_out.T, attn_out.T, ffn_down.T, ffn_in[0], ffn_in[1])
+    first_whole = lax.all_gather(pack(first_parts), "dp", axis=0, tiled=True)
+    second_whole = lax.all_gather(pack(second_parts), "dp", axis=0, tiled=True)
+    full_mamba_gate, full_mamba_mixer, full_bc, gathered_key_value, full_query, full_dt = unpack(
+        first_whole, [part.shape[1] for part in first_parts]
+    )
+    full_mamba_in = jnp.stack([full_mamba_gate, full_mamba_mixer])
+    out_t, attn_t, down_t, full_ffn_gate, full_ffn_up = unpack(
+        second_whole, [part.shape[1] for part in second_parts]
+    )
+    full_mamba_out, full_attn_out, full_ffn_down = out_t.T, attn_t.T, down_t.T
+    full_ffn_in = jnp.stack([full_ffn_gate, full_ffn_up])
     normed_own, pull_norm_one = jax.vjp(rms_rows, tokens.astype(jnp.float32), norm_gain)
     normed = spread(normed_own.astype(jnp.bfloat16))
     projected = jnp.einsum(
@@ -362,11 +370,11 @@
     squares = tensor_total(own_squares)
     mamba_norm, pull_gated = jax.vjp(gated_norm, gated, squares, gated_gain)
     mamba_low = mamba_norm.astype(jnp.bfloat16)
-    arrived = []
-    for distance in range(hops, 0, -1):
-        arrived.append(passed_along((key_rows, value_rows), "dp", distance))
-    all_keys = jnp.concatenate([piece[0] for piece in arrived] + [key_rows])
-    all_values = jnp.concatenate([piece[1] for piece in arrived] + [value_rows])
+    own_pair = jnp.concatenate([key_rows, value_rows], axis=1)
+    arrived = [passed_along(own_pair, "dp", distance) for distance in range(hops, 0, -1)]
+    all_pairs = jnp.concatenate(arrived + [own_pair])
+    all_keys = all_pairs[:, :HEAD_DIMENSION]
+    all_values = all_pairs[:, HEAD_DIMENSION:]
     output, row_lse = attend_block(queries, all_keys, all_values, block_mask(), scale)
     heads_out = output.reshape(group_rows, query_head_rows * HEAD_DIMENSION).astype(jnp.bfloat16)
     mixed_part = jnp.dot(mamba_low, full_mamba_out, preferred_element_type=jnp.float32)
@@ -384,7 +392,7 @@
         middle + summed_rows(jnp.dot(hidden, full_ffn_down, preferred_element_type=jnp.float32))
     ).astype(jnp.bfloat16)
     grad_full = spread(out_grad)
-    grad_ffn_down = jnp.einsum("tf,td->fd", hidden, grad_full, preferred_element_type=jnp.float32)
+    grad_ffn_down = jnp.einsum("td,tf->df", grad_full, hidden, preferred_element_type=jnp.float32)
     grad_hidden = jnp.einsum(
         "td,fd->tf", grad_full, full_ffn_down, preferred_element_type=jnp.float32
     )
@@ -405,10 +413,10 @@
     grad_middle = out_grad.astype(jnp.float32) + grad_middle_norm
     grad_mixed = spread(grad_middle.astype(jnp.bfloat16))
     grad_mamba_out = jnp.einsum(
-        "tc,td->cd", mamba_low, grad_mixed, preferred_element_type=jnp.float32
+        "td,tc->dc", grad_mixed, mamba_low, preferred_element_type=jnp.float32
     )
     grad_attn_out = jnp.einsum(
-        "tc,td->cd", heads_out, grad_mixed, preferred_element_type=jnp.float32
+        "td,tc->dc", grad_mixed, heads_out, preferred_element_type=jnp.float32
     )
     grad_mamba_norm = jnp.einsum(
         "td,cd->tc", grad_mixed, full_mamba_out, preferred_element_type=jnp.float32
@@ -461,20 +469,15 @@
     grad_query, grad_keys, grad_values = attend_back(
         queries, all_keys, all_values, block_mask(), scale, row_lse, grad_heads
     )
-    grad_keys_own = grad_keys[hops * group_rows :]
-    local_value_gradient = grad_values[hops * group_rows :]
+    grad_pairs = jnp.concatenate([grad_keys, grad_values], axis=1)
+    grad_pair_own = grad_pairs[hops * group_rows :]
     for distance in range(hops, 0, -1):
         slot = hops - distance
-        sent_back = passed_along(
-            (
-                grad_keys[slot * group_rows : (slot + 1) * group_rows],
-                grad_values[slot * group_rows : (slot + 1) * group_rows],
-            ),
-            "dp",
-            -distance,
+        grad_pair_own = grad_pair_own + passed_along(
+            grad_pairs[slot * group_rows : (slot + 1) * group_rows], "dp", -distance
         )
-        grad_keys_own = grad_keys_own + sent_back[0]
-        local_value_gradient = local_value_gradient + sent_back[1]
+    grad_keys_own = grad_pair_own[:, :HEAD_DIMENSION]
+    local_value_gradient = grad_pair_own[:, HEAD_DIMENSION:]
     grad_query_raw = rotary(grad_query, position, -1.0).reshape(group_rows, -1).astype(jnp.bfloat16)
     grad_key_raw = rotary(grad_keys_own[:, None, :], position, -1.0)[:, 0]
     key_value_gradient_full = jnp.zeros((group_rows, gathered_key_value.shape[1]), jnp.float32)
@@ -531,16 +534,33 @@
     grad_normed_own = summed_rows(grad_normed)
     grad_tokens_norm, grad_norm_gain = pull_norm_one(grad_normed_own)
     grad_tokens = grad_middle + grad_tokens_norm
+    late_parts = (
+        grad_mamba_in[0],
+        grad_mamba_in[1],
+        grad_bc_proj,
+        grad_kv_proj,
+        grad_query_proj,
+        grad_dt_proj,
+    )
+    early_parts = (grad_mamba_out, grad_attn_out, grad_ffn_down, grad_ffn_in[0], grad_ffn_in[1])
+    early = unpack(
+        lax.psum_scatter(pack(early_parts), "dp", scatter_dimension=0, tiled=True),
+        [part.shape[1] for part in early_parts],
+    )
+    late = unpack(
+        lax.psum_scatter(pack(late_parts), "dp", scatter_dimension=0, tiled=True),
+        [part.shape[1] for part in late_parts],
+    )
     scattered = (
-        lax.psum_scatter(grad_mamba_in, "dp", scatter_dimension=1, tiled=True),
-        lax.psum_scatter(grad_dt_proj, "dp", scatter_dimension=0, tiled=True),
-        lax.psum_scatter(grad_bc_proj, "dp", scatter_dimension=0, tiled=True),
-        lax.psum_scatter(grad_query_proj, "dp", scatter_dimension=0, tiled=True),
-        lax.psum_scatter(grad_kv_proj, "dp", scatter_dimension=0, tiled=True),
-        lax.psum_scatter(grad_mamba_out, "dp", scatter_dimension=1, tiled=True),
-        lax.psum_scatter(grad_attn_out, "dp", scatter_dimension=1, tiled=True),
-        lax.psum_scatter(grad_ffn_in, "dp", scatter_dimension=1, tiled=True),
-        lax.psum_scatter(grad_ffn_down, "dp", scatter_dimension=1, tiled=True),
+        jnp.stack(late[:2]),
+        late[5],
+        late[2],
+        late[4],
+        late[3],
+        early[0].T,
+        early[1].T,
+        jnp.stack(early[3:]),
+        early[2].T,
     )
 
     def widen(piece, axis_at):

time: 1690 us -> 1190 us (0.70)
  waiting for transfers between devices: 829 us -> 453 us
  blocking collectives: 277 us -> 96.9 us
  local copies, waits for them, and re-layouts: 187 us -> 229 us
  other arithmetic: 113 us -> 150 us
    reduce_scatter x9 -> x2, waiting for transfers between devices: 520 us -> 225 us  [the longest x1 147 us: per_device(): lax.psum_scatter(pack(early_parts), 'dp', scatter_dimension=0, tiled=True)]
    all_gather x6 -> x0, blocking collectives: 179 us -> none  [the longest x1 33.9 us: per_device(): lax.all_gather(bc_proj, 'dp', axis=0, tiled=True)]
    ppermute x20 -> x12, waiting for transfers between devices: 62 us -> 4.68 us  [passed_along(): lax.ppermute(value, axis, [(source, source + steps) for source in range(l...]
    all_gather x3 -> x2, waiting for transfers between devices: 89.7 us -> 47.5 us  [the longest x1 47.5 us: per_device(): first_whole = lax.all_gather(pack(first_parts), 'dp', axis=0, tiled=True)]
    ppermute x20 -> x12, starting transfers between devices: 45.2 us -> 29 us  [passed_along(): lax.ppermute(value, axis, [(source, source + steps) for source in range(l...]
  transfers between devices with their start and end apart: 42 -> 26, of which waited for: 25 -> 13; matrix products, arithmetic and copies ran while one was open for 22% -> 23% of each run, Pallas kernels for 0% -> 0%
where the time goes in v1:
time: 1190 us; the launch traced here: 1170 us
  waiting for transfers between devices  453 us (38%)
  local copies, waits for them, and re-layouts  229 us (19%)
  matrix products  182 us (15%)
  other arithmetic  150 us (13%)
  blocking collectives  96.9 us (8%)
  starting transfers between devices  30.2 us (3%)
  between operations  18.4 us (2%)
    reduce_scatter x1, waiting for transfers between devices, per_device(): lax.psum_scatter(pack(early_parts), 'dp', scatter_dimension=0, tiled=True)  147 us
    reduce_scatter x4, waiting for transfers between devices, summed_rows(): lax.psum_scatter(group_part, 'tensor', scatter_dimension=0, tiled=True)  87.8 us
    reduce_scatter x1, waiting for transfers between devices, per_device(): lax.psum_scatter(pack(late_parts), 'dp', scatter_dimension=0, tiled=True)  78.3 us
    all_gather x4, waiting for transfers between devices, spread(): return lax.all_gather(own_part, 'tensor', axis=0, tiled=True)  56.2 us
    dynamic_update_slice x8, local copies, waits for them, and re-layouts, local_scan(): lax.scan(jax.checkpoint(ssd_block), start_state, pieces)  47.6 us
    all_gather x1, waiting for transfers between devices, per_device(): first_whole = lax.all_gather(pack(first_parts), 'dp', axis=0, tiled=True)  47.5 us
    psum x1, blocking collectives, per_device(): lax.psum((grad_norm_gain, grad_ffn_gain, grad_conv_shared, widen(grad_con...  40.6 us
    squeeze x36, local copies, waits for them, and re-layouts, local_scan(): lax.scan(jax.checkpoint(ssd_block), start_state, pieces)  35 us
  transfers between devices with their start and end apart: 26, of which 13 were waited for; matrix products, arithmetic and copies ran while one was open for 23% of the time, Pallas kernels for 0%

profile of v1, /device:TPU:0, one launch (start us, length us, event | category | flops | bytes accessed | tf_op | source)
XLA Modules:
  0.0 1171.5 jit_solution(15718191914349827329)
XLA Ops:
  28.6 47.5 %all-gather.14.cloned.1.call-done = bf16[1024,1414]{0,1:T(8,128)(2,1)} async-done(((bf16[128,1414]{0,1:T(8,128)(2,1)}), bf16[1024,1414]{0,1:T(8,128)(2,1)}) %all-gather.14.cloned.1.call-update) | async-done | bytes 2895888 | tf_op jit(solution)/shard_map/all_gather | solution.py:292
  79.0 14.2 %all-gather.12.cloned.1.call-done = bf16[512,1024]{1,0:T(8,128)(2,1)} async-done(((bf16[128,1024]{1,0:T(8,128)(2,1)}), bf16[512,1024]{1,0:T(8,128)(2,1)}) %all-gather.12.cloned.1.call-update) | async-done | bytes 1048592 | tf_op jit(solution)/shard_map/all_gather | solution.py:249
  126.4 17.4 %all-reduce.20 = f32[48]{0:T(128)S(1)} all-reduce(f32[48]{0:T(128)S(1)} %multiply_dynamic-update-slice_fusion.1), channel_id=2, replica_groups=mesh['dp'=8,'tensor'=4] {'dp'}, use_global_device_ids=true, to_apply=%add.20 | all-reduce | flops 48 | bytes 384
  160.1 88.8 %while.69 = (s32[]{:T(128)}, f32[6,64,128]{2,1,0:T(8,128)S(1)}, f32[4,128,6,64]{1,0,3,2:T(4,128)}, f32[4,6,64,128]{3,2,1,0:T(8,128)}, f32[4,128,6]{2,1,0:T(8,128...) while((s32[]{:T(128)}, f32[6,64,128]{2,1,0:T(8,128)S(1)}, ...), condition=%wide.region_7.8_spmd.clone, body=%wide.region_5.7_spmd.clone.sunk | while | flops 252594944 | bytes 2862966 | solution.py:149
  174.3 6.0 dynamic_update_slice.107
  196.5 6.0 dynamic_update_slice.107
  218.7 6.0 dynamic_update_slice.107
  240.9 6.0 dynamic_update_slice.107
  269.4 30.8 %all-gather.24.cloned.1.call-done = f32[48,64,128]{2,1,0:T(8,128)} async-done(((f32[6,64,128]{2,1,0:T(8,128)}), f32[48,64,128]{2,1,0:T(8,128)}) %all-gather.24.cloned.1.call-update) | async-done | bytes 1572880 | tf_op jit(solution)/shard_map/all_gather | solution.py:25
  303.9 6.0 psum.84
  316.9 42.5 %reduce-scatter.7.cloned.1.call-done = f32[128,1024]{1,0:T(8,128)} async-done(((f32[512,1024]{1,0:T(8,128)}), f32[128,1024]{1,0:T(8,128)}) %reduce-scatter.7.cloned.1.call-update) | async-done | bytes 524304 | tf_op jit(solution)/shard_map/reduce_scatter | solution.py:252
  365.4 13.0 %all-gather.18.cloned.1.call-done = bf16[512,1024]{1,0:T(8,128)(2,1)} async-done(((bf16[128,1024]{1,0:T(8,128)(2,1)}), bf16[512,1024]{1,0:T(8,128)(2,1)}) %all-gather.18.cloned.1.call-update) | async-done | bytes 1048592 | tf_op jit(solution)/shard_map/all_gather | solution.py:249
  382.5 14.3 %all-gather.20.cloned.1.call-done = bf16[512,1024]{1,0:T(8,128)(2,1)} async-done(((bf16[128,1024]{1,0:T(8,128)(2,1)}), bf16[512,1024]{1,0:T(8,128)(2,1)}) %all-gather.20.cloned.1.call-update) | async-done | bytes 1048592 | tf_op jit(solution)/shard_map/all_gather | solution.py:249
  404.0 31.1 %reduce-scatter.11.cloned.1.call-done = f32[128,1024]{1,0:T(8,128)} async-done(((f32[512,1024]{1,0:T(8,128)}), f32[128,1024]{1,0:T(8,128)}) %reduce-scatter.11.cloned.1.call-update) | async-done | bytes 524304 | tf_op jit(solution)/shard_map/reduce_scatter | solution.py:252
  442.3 14.8 %all-gather.22.cloned.1.call-done = bf16[512,1024]{1,0:T(8,128)(2,1)} async-done(((bf16[128,1024]{1,0:T(8,128)(2,1)}), bf16[512,1024]{1,0:T(8,128)(2,1)}) %all-gather.22.cloned.1.call-update) | async-done | bytes 1048592 | tf_op jit(solution)/shard_map/all_gather | solution.py:249
  461.5 6.4 psum.85
  480.5 8.8 reduce-window.32
  495.1 6.4 fusion.163
  501.5 16.4 %convolution_bitcast_fusion.5 = f32[2560,64]{0,1:T(8,128)} fusion(f32[2560,512,2]{1,0,2:T(8,128)} %fusion.163, f32[2,512,2560]{1,2,0:T(8,128)} %copy-done, f32[2,512]{1,0:T(2,128)S(1)} %log_add_fusion, bf16[512,2,32]{0,2,1:T(8,128)(2,1)} %get-tuple-element.1081, bf16[512,2,32]{0,2,1:T(8,128)(2,1)} %get-tuple-element.1080), kind=kOutput, calls=%fused_computation.140 | convolution fusion | flops 362024448 | bytes 21762048 | tf_op jit(solution)/shard_map/gqk,qgd->kd/dot_general | solution.py:199
  517.9 5.8 fusion.81
  530.2 16.1 %fusion.96 = f32[512,2,64]{0,2,1:T(8,128)} fusion(f32[2560,512,2]{1,0,2:T(8,128)} %fusion.163, f32[2,512,2560]{1,2,0:T(8,128)} %copy-done, f32[2,512]{1,0:T(2,128)S(1)} %log_add_fusion, bf16[2560,128]{0,1:T(8,128)(2,1)} %copy-done.60), kind=kOutput, calls=%fused_computation.193 | convolution fusion | flops 361762304 | bytes 42541056 | tf_op jit(solution)/shard_map/gqk,kd->qgd/dot_general | solution.py:196
  562.8 12.4 %while.67 = (s32[]{:T(128)}, f32[6,64,128]{2,1,0:T(8,128)S(1)}, s32[]{:T(128)}, f32[8,6]{1,0:T(8,128)}, f32[8,6,64,128]{3,2,1,0:T(8,128)}, /*index=5*/s32[]{:T(128)}, s32[]{:T(128)}, s32[]{:T(128)}, s32[]{:T(128)}) while((s32[]{:T(128)}, f32[6,64,128]{2,1,0:T(8,128)S(1)}, s32[]{:T(128)}, f32[8,6]{1,0:T(8,128)}, ...), condition=%wide.region_27.28_spmd, body=%wide.region_26.27_spmd.sunk | while | flops 98310 | bytes 590051 | solution.py:34
  579.7 205.9 %while.68 = (s32[]{:T(128)}, f32[6,64,128]{2,1,0:T(8,128)S(1)}, f32[4,128,6,64]{1,0,3,2:T(4,128)}, f32[4,128,128]{2,1,0:T(8,128)}, f32[4,128,128]{2,1,0:T(8,128)...) while((s32[]{:T(128)}, f32[6,64,128]{2,1,0:T(8,128)S(1)}, ...), condition=%wide.region_38.39_spmd, body=%wide.region_28.38_spmd.sunk | while | flops 606566400 | bytes 7566515 | solution.py:149
  625.3 5.9 dynamic_update_slice.105
  676.8 5.9 dynamic_update_slice.105
  728.2 5.9 dynamic_update_slice.105
  779.7 5.9 dynamic_update_slice.105
  806.5 26.5 %all-reduce.24 = (bf16[512,256]{1,0:T(8,128)(2,1)}, bf16[512,256]{1,0:T(8,128)(2,1)}) all-reduce(f32[512,256]{1,0:T(8,128)} %copy-done.34, f32[512,256]{1,0:T(8,128)S(1)} %pad_maximum_fusion.10), channel_id=1, replica_groups=mesh['dp'=8,'tensor'=4] {'tensor'}, use_global_device_ids=true, to_apply=%region_45.46 | all-reduce | flops 262144 | bytes 1572864 | tf_op jit(solution)/shard_map/psum | solution.py:493
  865.9 14.1 %reduce-scatter.13.cloned.1.call-done = f32[128,1024]{1,0:T(8,128)} async-done(((f32[512,1024]{1,0:T(8,128)}), f32[128,1024]{1,0:T(8,128)}) %reduce-scatter.13.cloned.1.call-update) | async-done | bytes 524304 | tf_op jit(solution)/shard_map/reduce_scatter | solution.py:252
  881.3 40.6 %all-reduce.21 = (f32[1024]{0:T(1024)}, f32[4,1536]{1,0:T(4,128)S(1)}, f32[4,256]{1,0:T(4,128)}, f32[24]{0:T(128)S(1)}, f32[24]{0:T(128)S(1)}, /*index=5*/f32[24]{0:T(128)S(1)}, f32[1536]{0:T(1024)S(1)}, f32[1024]{0:T(1024)}) all-reduce(f32[1024]{0:T(1024)S(1)} %get-tuple-element.918, ...), channel_id=1, replica_groups=mesh['dp'=8,'tensor'=4] {'dp','tensor'}, use_global_device_ids=true, to_apply=%region_49.50 | all-reduce | flops 10824 | bytes 86592 | tf_op jit(solution)/shard_map/psum | solution.py:579
  927.3 78.3 %reduce-scatter.15.cloned.1.call-done = f32[128,1030]{0,1:T(8,128)} async-done(((f32[1024,1030]{0,1:T(8,128)}), f32[128,1030]{0,1:T(8,128)}) %reduce-scatter.15.cloned.1.call-update) | async-done | bytes 527376 | tf_op jit(solution)/shard_map/reduce_scatter | solution.py:551
  1011.9 146.9 %reduce-scatter.17.cloned.1.call-done = f32[128,2048]{0,1:T(8,128)} async-done(((f32[1024,2048]{0,1:T(8,128)}), f32[128,2048]{0,1:T(8,128)}) %reduce-scatter.17.cloned.1.call-update) | async-done | bytes 1048592 | tf_op jit(solution)/shard_map/reduce_scatter | solution.py:547
  (830 shorter events, 496.4 us)
Async XLA Ops:
  7.3 68.9 %all-gather.14.cloned.1.call-start = ((), (), s32[]{:S(2)}) async-start(), calls=%async_computation.7 | async-start | bytes 3262464 | tf_op jit(solution)/shard_map/all_gather | solution.py:292
  13.0 80.3 %all-gather.12.cloned.1.call-start = ((), (), s32[]{:S(2)}) async-start(), calls=%async_computation.6 | async-start | bytes 1310720 | tf_op jit(solution)/shard_map/all_gather | solution.py:249
  16.0 250.6 %all-gather.16.cloned.1.call-start = ((), (), s32[]{:S(2)}) async-start(), calls=%async_computation.8 | async-start | bytes 4718592 | tf_op jit(solution)/shard_map/all_gather | solution.py:293
  18.2 282.0 %all-gather.24.cloned.1.call-start = ((), (), s32[]{:S(2)}) async-start(), calls=%async_computation.18 | async-start | bytes 1769472 | tf_op jit(solution)/shard_map/all_gather | solution.py:25
  22.7 126.3 %copy-start.84 = (pred[512]{0:T(512)(128)(4,1)}, pred[512]{0:T(512)(128)(4,1)S(1)}, u32[]{:S(2)}) copy-start(pred[512]{0:T(512)(128)(4,1)S(1)} %get-tuple-element.1100) | copy-start | bytes 1540
  22.7 130.7 %copy-start.80 = (pred[512]{0:T(512)(128)(4,1)}, pred[512]{0:T(512)(128)(4,1)S(1)}, u32[]{:S(2)}) copy-start(pred[512]{0:T(512)(128)(4,1)S(1)} %get-tuple-element.1098) | copy-start | bytes 1540
  22.7 130.7 %copy-start.82 = (pred[512]{0:T(512)(128)(4,1)}, pred[512]{0:T(512)(128)(4,1)S(1)}, u32[]{:S(2)}) copy-start(pred[512]{0:T(512)(128)(4,1)S(1)} %get-tuple-element.1099) | copy-start | bytes 1540
  22.8 126.3 %copy-start.97 = (f32[1,256]{1,0:T(1,128)}, f32[1,256]{1,0:T(1,128)S(1)}, u32[]{:S(2)}) copy-start(f32[1,256]{1,0:T(1,128)S(1)} %get-tuple-element.1094) | copy-start | bytes 3076
  96.1 158.2 %collective-permute-start.5 = (bf16[512,128]{0,1:T(8,128)(2,1)}, bf16[512,128]{0,1:T(8,128)(2,1)}, u32[]{:S(2)}, u32[]{:S(2)}) collective-permute-start(bf16[512,128]{0,1:T(8,128)(2,1)} %pad_maximum_fusion.16), channel_id=1, source_target_pairs={{0,4},{4,8},{8,12},{12,16},{16,20},{20,24},{24,28},{1,5},{5,9},{9,... | collective-permute-start | bytes 393224 | tf_op jit(solution)/shard_map/ppermute | solution.py:40
  100.1 153.3 %collective-permute-start.4 = (bf16[512,128]{0,1:T(8,128)(2,1)}, bf16[512,128]{0,1:T(8,128)(2,1)}, u32[]{:S(2)}, u32[]{:S(2)}) collective-permute-start(bf16[512,128]{0,1:T(8,128)(2,1)} %pad_maximum_fusion.16), channel_id=1, source_target_pairs={{0,8},{4,12},{8,16},{12,20},{16,24},{20,28},{1,9},{5,13},{9,17},{1... | collective-permute-start | bytes 393224 | tf_op jit(solution)/shard_map/ppermute | solution.py:40
  103.5 148.9 %collective-permute-start.3 = (bf16[512,128]{0,1:T(8,128)(2,1)}, bf16[512,128]{0,1:T(8,128)(2,1)}, u32[]{:S(2)}, u32[]{:S(2)}) collective-permute-start(bf16[512,128]{0,1:T(8,128)(2,1)} %pad_maximum_fusion.16), channel_id=1, source_target_pairs={{0,12},{4,16},{8,20},{12,24},{16,28},{1,13},{5,17},{9,21},{13,25},... | collective-permute-start | bytes 393224 | tf_op jit(solution)/shard_map/ppermute | solution.py:40
  107.9 143.7 %collective-permute-start.2 = (bf16[512,128]{0,1:T(8,128)(2,1)}, bf16[512,128]{0,1:T(8,128)(2,1)}, u32[]{:S(2)}, u32[]{:S(2)}) collective-permute-start(bf16[512,128]{0,1:T(8,128)(2,1)} %pad_maximum_fusion.16), channel_id=1, source_target_pairs={{0,16},{4,20},{8,24},{12,28},{1,17},{5,21},{9,25},{13,29},{2,18},{... | collective-permute-start | bytes 393224 | tf_op jit(solution)/shard_map/ppermute | solution.py:40
  119.3 26.1 %collective-permute-start.1 = (bf16[3,256]{1,0:T(4,128)(2,1)S(1)}, bf16[3,256]{1,0:T(4,128)(2,1)S(1)}, u32[]{:S(2)}, u32[]{:S(2)}) collective-permute-start(bf16[3,256]{1,0:T(4,128)(2,1)S(1)} %slice.422), channel_id=1, source_target_pairs={{0,4},{4,8},{8,12},{12,16},{16,20},{20,24},{24,28},{1,5},{5,9},{9,... | collective-permute-start | bytes 4616 | tf_op jit(solution)/shard_map/ppermute | solution.py:40
  145.3 7.8 collective-permute-start
  251.3 108.0 %reduce-scatter.7.cloned.1.call-start = ((), (), s32[]{:S(2)}) async-start(), calls=%async_computation.9 | async-start | bytes 2621440 | tf_op jit(solution)/shard_map/reduce_scatter | solution.py:252
  300.2 274.9 %copy-start.5 = (f32[6,64,128]{2,1,0:T(8,128)}, f32[6,64,128]{2,1,0:T(8,128)S(1)}, u32[]{:S(2)}) copy-start(f32[6,64,128]{2,1,0:T(8,128)S(1)} %get-tuple-element.580) | copy-start | bytes 589828
  309.9 158.1 %copy-start.75 = (f32[512]{0:T(512)}, f32[512]{0:T(512)S(1)}, u32[]{:S(2)}) copy-start(f32[512]{0:T(512)S(1)} %fusion.201) | copy-start | bytes 6148
  316.8 61.6 %all-gather.18.cloned.1.call-start = ((), (), s32[]{:S(2)}) async-start(), calls=%async_computation.10 | async-start | bytes 1310720 | tf_op jit(solution)/shard_map/all_gather | solution.py:249
  361.5 35.3 %all-gather.20.cloned.1.call-start = ((), (), s32[]{:S(2)}) async-start(), calls=%async_computation.12 | async-start | bytes 1310720 | tf_op jit(solution)/shard_map/all_gather | solution.py:249
  362.3 72.9 %reduce-scatter.11.cloned.1.call-start = ((), (), s32[]{:S(2)}) async-start(), calls=%async_computation.13 | async-start | bytes 2621440 | tf_op jit(solution)/shard_map/reduce_scatter | solution.py:252
  403.6 53.5 %all-gather.22.cloned.1.call-start = ((), (), s32[]{:S(2)}) async-start(), calls=%async_computation.14 | async-start | bytes 1310720 | tf_op jit(solution)/shard_map/all_gather | solution.py:249
  440.1 121.9 %all-gather.26.cloned.1.call-start = ((), (), s32[]{:S(2)}) async-start(), calls=%async_computation.19 | async-start | bytes 1769472 | tf_op jit(solution)/shard_map/all_gather | solution.py:25
  480.5 399.5 %reduce-scatter.13.cloned.1.call-start = ((), (), s32[]{:S(2)}) async-start(), calls=%async_computation.15 | async-start | bytes 2621440 | tf_op jit(solution)/shard_map/reduce_scatter | solution.py:252
  524.8 26.7 %collective-permute-start.8 = (f32[512,128]{0,1:T(8,128)}, f32[512,128]{0,1:T(8,128)}, u32[]{:S(2)}, u32[]{:S(2)}) collective-permute-start(f32[512,128]{0,1:T(8,128)} %get-tuple-element.1051), channel_id=1, source_target_pairs={{16,0},{20,4},{24,8},{28,12},{17,1},{21,5},{25,9},{29,13},{18,2},{... | collective-permute-start | bytes 786440 | tf_op jit(solution)/shard_map/ppermute | solution.py:40
  526.1 25.4 %collective-permute-start.9 = (f32[512,128]{0,1:T(8,128)}, f32[512,128]{0,1:T(8,128)}, u32[]{:S(2)}, u32[]{:S(2)}) collective-permute-start(f32[512,128]{0,1:T(8,128)} %get-tuple-element.1052), channel_id=1, source_target_pairs={{12,0},{16,4},{20,8},{24,12},{28,16},{13,1},{17,5},{21,9},{25,13},... | collective-permute-start | bytes 786440 | tf_op jit(solution)/shard_map/ppermute | solution.py:40
  527.4 24.1 %collective-permute-start.11 = (f32[512,128]{0,1:T(8,128)}, f32[512,128]{0,1:T(8,128)}, u32[]{:S(2)}, u32[]{:S(2)}) collective-permute-start(f32[512,128]{0,1:T(8,128)} %get-tuple-element.1053), channel_id=1, source_target_pairs={{4,0},{8,4},{12,8},{16,12},{20,16},{24,20},{28,24},{5,1},{9,5},{13... | collective-permute-start | bytes 786440 | tf_op jit(solution)/shard_map/ppermute | solution.py:40
  528.7 25.5 %collective-permute-start.10 = (f32[512,128]{0,1:T(8,128)}, f32[512,128]{0,1:T(8,128)}, u32[]{:S(2)}, u32[]{:S(2)}) collective-permute-start(f32[512,128]{0,1:T(8,128)} %get-tuple-element.1054), channel_id=1, source_target_pairs={{8,0},{12,4},{16,8},{20,12},{24,16},{28,20},{9,1},{13,5},{17,9},{2... | collective-permute-start | bytes 786440 | tf_op jit(solution)/shard_map/ppermute | solution.py:40
  796.9 9.6 collective-permute-start.7
  802.0 34.1 %collective-permute-start.6 = (f32[3,384]{0,1:T(8,128)S(1)}, f32[3,384]{0,1:T(8,128)}, u32[]{:S(2)}, u32[]{:S(2)}) collective-permute-start(f32[3,384]{0,1:T(8,128)S(1)} %pad_add_fusion.2), channel_id=1, source_target_pairs={{4,0},{8,4},{12,8},{16,12},{20,16},{24,20},{28,24},{5,1},{9,5},{13... | collective-permute-start | bytes 13832 | tf_op jit(solution)/shard_map/ppermute | solution.py:40
  841.2 83.7 %reduce-scatter.9.cloned.1.call-start = ((), (), s32[]{:S(2)}) async-start(), calls=%async_computation.11 | async-start | bytes 2621440 | tf_op jit(solution)/shard_map/reduce_scatter | solution.py:252
  845.0 160.7 %reduce-scatter.15.cloned.1.call-start = ((), (), s32[]{:S(2)}) async-start(), calls=%async_computation.16 | async-start | bytes 4755456 | tf_op jit(solution)/shard_map/reduce_scatter | solution.py:551
  852.8 306.0 %reduce-scatter.17.cloned.1.call-start = ((), (), s32[]{:S(2)}) async-start(), calls=%async_computation.17 | async-start | bytes 9437184 | tf_op jit(solution)/shard_map/reduce_scatter | solution.py:547
  (143 other events, 2373.0 us)
Sparse Core Ops, SparseCore 0:
  13.1 63.0 all-gather.13
  78.3 14.9 all-gather.11
  95.3 88.3 all-gather.15
  251.4 48.7 all-gather.23
  316.9 42.3 reduce-scatter.6
  361.6 16.7 all-gather.17
  380.0 16.7 all-gather.19
  403.7 31.4 reduce-scatter.10
  440.3 16.7 all-gather.21
  480.6 45.2 all-gather.25
  841.3 38.6 reduce-scatter.12
  882.6 31.5 reduce-scatter.8
  917.8 87.8 reduce-scatter.14
  1009.5 149.1 reduce-scatter.16
